TPU v7x, 32 devices: a whole 2x2x4 slice. The times are simulated.
32 devices in a mesh: group: 2 (over x), tensor: 4 (over z), rep: 4 (over y, core).
Axes of the slice: x: 2, y: 2, z: 4, core: 2. Of those that a mesh axis runs over, the one named last changes fastest.
Arguments:
- probe_vectors: bfloat16 [128, 64, 128], P(('group', 'rep'), 'tensor'), may hold values from -500 to 500
- stored_lookup_vectors: bfloat16 [128, 8, 512, 128], P(('group', 'rep'), 'tensor'), may hold values from -6 to 6
- stored_content_vectors: bfloat16 [128, 8, 512, 128], P(('group', 'rep'), 'tensor'), may hold values from -6 to 6
- fresh_lookup_vector: bfloat16 [128, 8, 128], P(('group', 'rep'), 'tensor'), may hold values from -6 to 6
- fresh_content_vector: bfloat16 [128, 8, 128], P(('group', 'rep'), 'tensor'), may hold values from -6 to 6
- history_counts: int32 [128], P(('group', 'rep')), may hold values from 1 to 512, as said below
- mixing_matrix: bfloat16 [8192, 8192], P('tensor', ('group', 'rep')), may hold values from -0.25 to 0.25
- skip_stream: bfloat16 [128, 8192], P(('group', 'rep'), 'tensor'), may hold values from -8 to 8
- closing_multiplier: bfloat16 [8192], P('tensor'), may hold values from 0.25 to 1.75
- lexicon_matrix: bfloat16 [8192, 16384], P(None, ('group', 'tensor', 'rep')), may hold values from -0.088388348 to 0.088388348
- sharpening_factor: float32 [128], replicated, may hold values from 0.5 to 20
- desired_perplexity: float32 [128], replicated, may hold values from 6 to 12
- chosen_symbols: int32 [128], replicated, may hold values from 0 to 16383
Outputs:
- hidden: bfloat16 [128, 8192], P(('group', 'rep'), 'tensor')
- next_targets: float32 [128], replicated
- surprise: float32 [128], replicated
Inputs may be any that keep to these rules, and one draw needn't show every extreme that they name: `history_counts`: each row holds at least one cached position; some row holds 512.
All inputs are finite; a program needn't handle non-finite values.
Results may differ from a plain program's by a relative error of at most 0.0063.
Values may be sent and summed in bfloat16 or wider, within the bound.
A program may use at most 128 MiB of HBM per device.

v0:
```python
import math

import jax
import jax.numpy as jnp
from jax import lax
from jax.sharding import PartitionSpec as P

cut_slope = 4.0


def attend(
    probe_vectors,
    stored_lookup_vectors,
    stored_content_vectors,
    fresh_lookup_vector,
    fresh_content_vector,
    history_counts,
):
    rows, kv_local, cache_len, head_dim = stored_lookup_vectors.shape
    heads_local = probe_vectors.shape[1]
    grouped_query_rows = probe_vectors.reshape(rows, kv_local, heads_local // kv_local, head_dim)
    score_scale = 1.0 / math.sqrt(head_dim)
    self_entry = (
        jnp.einsum(
            "mjqo,mjo->mjq",
            grouped_query_rows,
            fresh_lookup_vector,
            preferred_element_type=jnp.float32,
        )
        * score_scale
    )
    scores = (
        jnp.einsum(
            "bkgd,bkld->bkgl",
            grouped_query_rows,
            stored_lookup_vectors,
            preferred_element_type=jnp.float32,
        )
        * score_scale
    )
    position = lax.broadcasted_iota(jnp.int32, (1, 1, 1, cache_len), 3)
    live = position < history_counts[:, None, None, None]
    top = jnp.maximum(jnp.max(jnp.where(live, scores, -1e30), axis=3), self_entry)
    expo = jnp.where(live, jnp.exp(scores - top[..., None]), 0.0)
    total = jnp.sum(expo, axis=3)
    accum = jnp.einsum(
        "bkgl,bkld->bkgd",
        expo.astype(jnp.bfloat16),
        stored_content_vectors,
        preferred_element_type=jnp.float32,
    )
    own_expo = jnp.exp(self_entry - top)
    total = total + own_expo
    accum = accum + jnp.einsum(
        "vct,vcn->vctn",
        own_expo.astype(jnp.bfloat16),
        fresh_content_vector,
        preferred_element_type=jnp.float32,
    )
    return (accum / total[..., None]).reshape(rows, heads_local * head_dim).astype(jnp.bfloat16)


def shards(
    probe_vectors,
    stored_lookup_vectors,
    stored_content_vectors,
    fresh_lookup_vector,
    fresh_content_vector,
    history_counts,
    mixing_matrix,
    skip_stream,
    closing_multiplier,
    lexicon_matrix,
    sharpening_factor,
    desired_perplexity,
    chosen_symbols,
):
    attn = attend(
        probe_vectors,
        stored_lookup_vectors,
        stored_content_vectors,
        fresh_lookup_vector,
        fresh_content_vector,
        history_counts,
    )
    every_attn = lax.all_gather(attn, ("group", "rep"), axis=0, tiled=True)
    partial_cols = jnp.dot(every_attn, mixing_matrix, preferred_element_type=jnp.float32)
    terms = lax.all_to_all(partial_cols, ("group", "rep"), split_axis=0, concat_axis=1, tiled=True)
    summed = lax.psum_scatter(terms, "tensor", scatter_dimension=1, tiled=True)
    hidden = (skip_stream.astype(jnp.float32) + summed).astype(jnp.bfloat16)
    wide = hidden.astype(jnp.float32)
    squares = lax.psum(jnp.sum(wide * wide, axis=1), "tensor")
    width = wide.shape[1] * lax.axis_size("tensor")
    rescaled_stream = (
        wide * lax.rsqrt(squares / width + 1e-05)[:, None] * closing_multiplier.astype(jnp.float32)
    ).astype(jnp.bfloat16)
    features = lax.all_gather(rescaled_stream, "tensor", axis=1, tiled=True)
    unnormalized_odds = (
        jnp.dot(
            lax.all_gather(features, ("group", "rep"), axis=0, tiled=True),
            lexicon_matrix,
            preferred_element_type=jnp.float32,
        )
        * sharpening_factor[:, None]
    )
    vocab_local = lexicon_matrix.shape[1]
    offset = lax.axis_index(("group", "tensor", "rep")) * vocab_local
    entry_ids = offset + lax.broadcasted_iota(jnp.int32, (1, vocab_local), 1)
    token_part = jnp.sum(
        jnp.where(entry_ids == chosen_symbols[:, None], unnormalized_odds, 0.0), axis=1
    )
    top = lax.pmax(jnp.max(unnormalized_odds, axis=1), ("group", "tensor", "rep"))
    local_total = jnp.sum(jnp.exp(unnormalized_odds - top[:, None]), axis=1)
    total, token_logit = lax.psum((local_total, token_part), ("group", "tensor", "rep"))
    lognorm = top + jnp.log(total)
    logp = unnormalized_odds - lognorm[:, None]
    bits = -logp / math.log(2.0)
    logw = logp + jax.nn.log_sigmoid(cut_slope * (desired_perplexity[:, None] - bits))
    kept = lax.psum(jnp.sum(jnp.exp(logw), axis=1), ("group", "tensor", "rep"))
    token_logp = token_logit - lognorm
    token_logw = token_logp + jax.nn.log_sigmoid(
        cut_slope * (desired_perplexity + token_logp / math.log(2.0))
    )
    surprise = -(token_logw - jnp.log(kept)) / math.log(2.0)
    next_targets = desired_perplexity - 0.1 * (surprise - 5.0)
    return (hidden, next_targets, surprise)


def solution(mesh):
    placed = (
        P(("group", "rep"), "tensor", None),
        P(("group", "rep"), "tensor", None, None),
        P(("group", "rep"), "tensor", None, None),
        P(("group", "rep"), "tensor", None),
        P(("group", "rep"), "tensor", None),
        P(("group", "rep")),
        P("tensor", ("group", "rep")),
        P(("group", "rep"), "tensor"),
        P("tensor"),
        P(None, ("group", "tensor", "rep")),
        P(),
        P(),
        P(),
    )
    return jax.shard_map(
        shards,
        mesh=mesh,
        in_specs=placed,
        out_specs=(P(("group", "rep"), "tensor"), P(), P()),
        check_vma=False,
    )
```

profile of v0, /device:TPU:0, one launch (start us, length us, event | category | flops | bytes accessed | tf_op | source)
XLA Modules:
  0.0 245.3 jit_solution(16571055939812468116)
XLA Ops:
  7.2 0.0 copy-start
  7.2 0.0 copy-start.4
  7.2 0.0 reduce-scatter.2.cloned.1.call-start
  7.2 0.0 copy-start.8
  7.2 0.9 iota_compare_fusion
  8.1 0.0 copy-done
  8.1 1.1 fusion.15
  9.2 3.5 %select_reduce_fusion = (f32[16,2,8]{2,1,0:T(2,128)S(1)}, f32[16,2,8,512]{3,2,1,0:T(8,128)S(1)}) fusion(pred[16,512]{1,0:T(8,128)(4,1)S(1)} %iota_compare_fusion, bf16[16,2,512,128]{3,2,1,0:T(8,128)(2,1)} %param.14, bf16[16,16,128]{2,1,0:T(8,128)(2,1)S(1)} %copy-done), kind=kOutput, calls=%fused_computation.7 | convolution fusion | flops 33947392 | bytes 4793344 | tf_op jit(solution)/shard_map/bkgd,bkld->bkgl/dot_general | solution.py:33
  12.7 0.0 copy-start.1
  12.7 0.3 fusion.2
  13.0 0.0 copy-done.4
  13.0 0.0 copy-done.8
  13.0 0.7 fusion.1
  13.8 0.0 copy-start.5
  13.8 0.0 copy-start.3
  13.8 11.4 %all_gather.9 = bf16[128,2048]{1,0:T(8,128)(2,1)S(1)} all-gather(bf16[16,2048]{1,0:T(8,128)(2,1)S(1)} %bitcast.28), channel_id=1, replica_groups=mesh['group'=2,'tensor'=4,'rep'=4] {'group','rep'}, dimensions={0}, use_global_device_ids=true | all-gather | bytes 589824 | tf_op jit(solution)/shard_map/all_gather | solution.py:86
  25.3 0.0 copy-done.1
  25.3 0.0 copy-start.6
  25.3 0.7 fusion.24
  26.0 11.5 %all_to_all.19 = f32[8,16,1024]{2,1,0:T(8,128)S(1)} all-to-all(f32[8,16,1024]{2,1,0:T(8,128)S(1)} %bitcast.25), channel_id=1, replica_groups=mesh['group'=2,'tensor'=4,'rep'=4] {'group','rep'}, dimensions={0} | all-to-all | bytes 1048576 | tf_op jit(solution)/shard_map/all_to_all | solution.py:88
  37.5 0.8 copy.19
  38.3 0.0 reduce-scatter.2.cloned.1.call-update
  38.3 0.0 all-gather.2.cloned.1.call-start
  38.4 0.0 copy-done.5
  38.4 22.0 %reduce-scatter.2.cloned.1.call-done = f32[16,2048]{1,0:T(8,128)} async-done(((f32[16,8192]{1,0:T(8,128)}), f32[16,2048]{1,0:T(8,128)}) %reduce-scatter.2.cloned.1.call-update) | async-done | bytes 131088 | tf_op jit(solution)/shard_map/reduce_scatter | solution.py:89
  60.4 0.0 copy-done.3
  60.4 1.0 fusion.12
  61.5 0.0 copy-start.2
  61.5 8.7 %psum.28 = f32[16]{0:T(128)S(1)} all-reduce(f32[16]{0:T(128)S(1)} %get-tuple-element.9), channel_id=1, replica_groups=mesh['group'=2,'tensor'=4,'rep'=4] {'tensor'}, use_global_device_ids=true, to_apply=%region_4.5 | all-reduce | flops 16 | bytes 128 | tf_op jit(solution)/shard_map/psum | solution.py:92
  70.2 0.1 fusion.14
  70.3 14.5 %all_gather.10 = bf16[16,8192]{1,0:T(8,128)(2,1)} all-gather(bf16[16,2048]{1,0:T(8,128)(2,1)S(1)} %fusion.14), channel_id=1, replica_groups=mesh['group'=2,'tensor'=4,'rep'=4] {'tensor'}, dimensions={1}, use_global_device_ids=true | all-gather | bytes 327680 | tf_op jit(solution)/shard_map/all_gather | solution.py:97
  84.8 0.0 all-gather.2.cloned.1.call-update
  84.9 0.0 copy-start.7
  84.9 0.0 copy-start.9
  84.9 27.5 %all-gather.2.cloned.1.call-done = bf16[128,8192]{1,0:T(8,128)(2,1)} async-done(((bf16[16,8192]{1,0:T(8,128)(2,1)}), bf16[128,8192]{1,0:T(8,128)(2,1)}) %all-gather.2.cloned.1.call-update) | async-done | bytes 2097168 | tf_op jit(solution)/shard_map/all_gather | solution.py:100
  112.4 0.0 copy-done.6
  112.4 5.4 %fusion.23 = (f32[128]{0:T(128)S(1)}, f32[128,512]{1,0:T(8,128)S(1)}) fusion(f32[128]{0:T(128)S(1)} %copy-done.6, bf16[128,8192]{1,0:T(8,128)(2,1)} %all-gather.2.cloned.1.call-done, bf16[8192,512]{1,0:T(8,128)(2,1)} %param.22), kind=kOutput, calls=%fused_computation.44 | convolution fusion | flops 1073872768 | bytes 10748928 | tf_op jit(solution)/shard_map/dot_general | solution.py:99
  117.8 0.0 copy-done.2
  117.8 39.4 %pmax.7 = f32[128]{0:T(128)S(1)} all-reduce(f32[128]{0:T(128)S(1)} %get-tuple-element.15), channel_id=1, replica_groups=mesh['group'=2,'tensor'=4,'rep'=4] {'group','tensor','rep'}, use_global_device_ids=true, to_apply=%region_8.9 | all-reduce | flops 128 | bytes 1024 | tf_op jit(solution)/shard_map/pmax | solution.py:112
  157.2 0.2 exponential_reduce_fusion
  157.3 41.0 %psum.30 = f32[128]{0:T(128)S(1)} all-reduce(f32[128]{0:T(128)S(1)} %exponential_reduce_fusion), channel_id=1, replica_groups=mesh['group'=2,'tensor'=4,'rep'=4] {'group','tensor','rep'}, use_global_device_ids=true, to_apply=%region_10.11 | all-reduce | flops 128 | bytes 1024 | tf_op jit(solution)/shard_map/psum | solution.py:114
  198.4 0.0 copy-done.7
  198.4 0.0 copy-done.9
  198.4 0.4 select_reduce_fusion.1
  198.8 39.1 %all-reduce = (f32[128]{0:T(128)S(1)}, f32[128]{0:T(128)S(1)}) all-reduce(f32[128]{0:T(128)S(1)} %get-tuple-element.4, f32[128]{0:T(128)S(1)} %get-tuple-element.3), channel_id=1, replica_groups=mesh['group'=2,'tensor'=4,'rep'=4] {'group','tensor','rep'}, use_global_device_ids=true, to_apply=%region_12.13 | all-reduce | flops 256 | bytes 2048 | tf_op jit(solution)/shard_map/psum | solution.py:119
  237.9 0.5 multiply_subtract_fusion
  (8 shorter events, 0.1 us)
Async XLA Ops:
  7.2 1.0 copy-start
  7.2 5.8 %copy-start.4 = (bf16[16,2,128]{2,1,0:T(2,128)(2,1)S(1)}, bf16[16,2,128]{2,1,0:T(2,128)(2,1)}, u32[]{:S(2)}) copy-start(bf16[16,2,128]{2,1,0:T(2,128)(2,1)} %param.17) | copy-start | bytes 24580
  7.2 53.2 %reduce-scatter.2.cloned.1.call-start = ((), (), s32[]{:S(2)}) async-start(), calls=%async_computation.2 | async-start | bytes 655360 | tf_op jit(solution)/shard_map/reduce_scatter | solution.py:89
  7.2 5.8 %copy-start.8 = (bf16[16,2,512,128]{3,2,1,0:T(8,128)(2,1)S(1)}, bf16[16,2,512,128]{3,2,1,0:T(8,128)(2,1)}, u32[]{:S(2)}) copy-start(bf16[16,2,512,128]{3,2,1,0:T(8,128)(2,1)} %param.15) | copy-start | bytes 12582916
  12.7 12.6 %copy-start.1 = (bf16[2048,1024]{1,0:T(8,128)(2,1)S(1)}, bf16[2048,1024]{1,0:T(8,128)(2,1)}, u32[]{:S(2)}) copy-start(bf16[2048,1024]{1,0:T(8,128)(2,1)} %param.19) | copy-start | bytes 12582916
  13.8 24.6 %copy-start.5 = (bf16[2048]{0:T(1024)(128)(2,1)S(1)}, bf16[2048]{0:T(1024)(128)(2,1)}, u32[]{:S(2)}) copy-start(bf16[2048]{0:T(1024)(128)(2,1)} %param.21) | copy-start | bytes 12292
  13.8 46.6 %copy-start.3 = (bf16[16,2048]{1,0:T(8,128)(2,1)S(1)}, bf16[16,2048]{1,0:T(8,128)(2,1)}, u32[]{:S(2)}) copy-start(bf16[16,2048]{1,0:T(8,128)(2,1)} %param.20) | copy-start | bytes 196612
  25.3 87.1 %copy-start.6 = (f32[128]{0:T(128)S(1)}, f32[128]{0:T(128)}, u32[]{:S(2)}) copy-start(f32[128]{0:T(128)} %param.23) | copy-start | bytes 1540
  38.3 74.1 %all-gather.2.cloned.1.call-start = ((), (), s32[]{:S(2)}) async-start(), calls=%async_computation.3 | async-start | bytes 2359296 | tf_op jit(solution)/shard_map/all_gather | solution.py:100
  61.5 56.3 %copy-start.2 = (bf16[16,2048]{1,0:T(8,128)(2,1)}, bf16[16,2048]{1,0:T(8,128)(2,1)S(1)}, u32[]{:S(2)}) copy-start(bf16[16,2048]{1,0:T(8,128)(2,1)S(1)} %get-tuple-element.10) | copy-start | bytes 196612
  84.9 113.5 %copy-start.7 = (f32[128]{0:T(128)S(1)}, f32[128]{0:T(128)}, u32[]{:S(2)}) copy-start(f32[128]{0:T(128)} %param.24) | copy-start | bytes 1540
  84.9 113.5 %copy-start.9 = (s32[128]{0:T(128)S(1)}, s32[128]{0:T(128)}, u32[]{:S(2)}) copy-start(s32[128]{0:T(128)} %param.25) | copy-start | bytes 1540
Sparse Core Ops, SparseCore 0:
  38.5 21.9 reduce-scatter.1
  85.0 27.3 all-gather.1
where the time goes:
time: 246 us; the launch traced here: 245 us
  blocking collectives  166 us (67%)
  waiting for transfers between devices  49.6 us (20%)
  between operations  14.2 us (6%)
  matrix products  11.3 us (5%)
  other arithmetic  3.48 us (1%)
    psum x1, blocking collectives, shards(): lax.psum((local_total, token_part), ('group', 'tensor', 'rep'))  41 us
    pmax x1, blocking collectives, shards(): lax.pmax(jnp.max(unnormalized_odds, axis=1), ('group', 'tensor', 'rep'))  39.4 us
    psum x1, blocking collectives, shards(): kept = lax.psum(jnp.sum(jnp.exp(logw), axis=1), ('group', 'tensor', 'rep'))  39.1 us
    all_gather x1, waiting for transfers between devices, shards(): lax.all_gather(features, ('group', 'rep'), axis=0, tiled=True)  27.5 us
    reduce_scatter x1, waiting for transfers between devices, shards(): summed = lax.psum_scatter(terms, 'tensor', scatter_dimension=1, tiled=True)  22 us
    all_gather x1, blocking collectives, shards(): features = lax.all_gather(rescaled_stream, 'tensor', axis=1, tiled=True)  14.5 us
    all_to_all x1, blocking collectives, shards(): lax.all_to_all(partial_cols, ('group', 'rep'), split_axis=0, concat_axis=...  11.5 us
    all_gather x1, blocking collectives, shards(): every_attn = lax.all_gather(attn, ('group', 'rep'), axis=0, tiled=True)  11.4 us
  transfers between devices with their start and end apart: 2, of which 2 were waited for; matrix products, arithmetic and copies ran while one was open for 0% of the time, Pallas kernels for 0%

commit v1 on v0

v1 whole, which is shorter than its diff:
```python
import functools
import math

import jax
import jax.numpy as jnp
from jax import lax
from jax.experimental import pallas as pl
from jax.experimental.pallas import tpu as pltpu
from jax.sharding import PartitionSpec as P

cut_slope = 4.0
MESH = pl.DeviceIdType.MESH


def attend(
    probe_vectors,
    stored_lookup_vectors,
    stored_content_vectors,
    fresh_lookup_vector,
    fresh_content_vector,
    history_counts,
):
    rows, kv_local, cache_len, head_dim = stored_lookup_vectors.shape
    heads_local = probe_vectors.shape[1]
    grouped_query_rows = probe_vectors.reshape(rows, kv_local, heads_local // kv_local, head_dim)
    score_scale = 1.0 / math.sqrt(head_dim)
    self_entry = (
        jnp.einsum(
            "mjqo,mjo->mjq",
            grouped_query_rows,
            fresh_lookup_vector,
            preferred_element_type=jnp.float32,
        )
        * score_scale
    )
    scores = (
        jnp.einsum(
            "bkgd,bkld->bkgl",
            grouped_query_rows,
            stored_lookup_vectors,
            preferred_element_type=jnp.float32,
        )
        * score_scale
    )
    position = lax.broadcasted_iota(jnp.int32, (1, 1, 1, cache_len), 3)
    live = position < history_counts[:, None, None, None]
    top = jnp.maximum(jnp.max(jnp.where(live, scores, -1e30), axis=3), self_entry)
    expo = jnp.where(live, jnp.exp(scores - top[..., None]), 0.0)
    total = jnp.sum(expo, axis=3)
    accum = jnp.einsum(
        "bkgl,bkld->bkgd",
        expo.astype(jnp.bfloat16),
        stored_content_vectors,
        preferred_element_type=jnp.float32,
    )
    own_expo = jnp.exp(self_entry - top)
    total = total + own_expo
    accum = accum + jnp.einsum(
        "vct,vcn->vctn",
        own_expo.astype(jnp.bfloat16),
        fresh_content_vector,
        preferred_element_type=jnp.float32,
    )
    return (accum / total[..., None]).reshape(rows, heads_local * head_dim).astype(jnp.bfloat16)


axes = ("group", "tensor", "rep")


def local_wait(ref, sem):
    pltpu.make_async_copy(ref, ref, sem).wait()


def tail_kernel(
    sizes,
    attn_ref,
    mixing_hbm,
    skip_ref,
    gain_ref,
    lexicon_hbm,
    sharp_ref,
    mu_ref,
    chosen_ref,
    hidden_ref,
    targets_ref,
    surprise_ref,
    mixing,
    lexicon,
    every_attn,
    part,
    outgoing,
    incoming,
    skip_block,
    gains,
    state,
    logits,
    squares,
    stats,
    kept_parts,
    load_sems,
    attn_send,
    attn_recv,
    skip_send,
    skip_recv,
    gain_send,
    gain_recv,
    part_send,
    part_recv,
    column_send,
    plane_send,
    pair_send,
    state_recv,
    stats_sems,
    kept_sems,
):
    G, T, R = sizes
    N = G * T * R
    columns = G * R
    fold = columns // T
    pairs = R // 2
    own_rows = attn_ref.shape[0]
    rows = every_attn.shape[0]
    block_rows = rows // T
    width = mixing.shape[1]
    vocab_local = lexicon.shape[1]

    g, t, r = (lax.axis_index(a) for a in axes)
    pair, core = r // 2, r % 2
    other = 1 - core
    column = g * R + r
    twin = g * R + pair * 2 + other
    me = (g * T + t) * R + r

    load_mixing = pltpu.make_async_copy(mixing_hbm, mixing, load_sems.at[0])
    load_lexicon = pltpu.make_async_copy(lexicon_hbm, lexicon, load_sems.at[1])
    load_mixing.start()
    load_lexicon.start()

    def device_of(index):
        return (index // (T * R), (index // R) % T, index % R)

    barrier = pltpu.get_barrier_semaphore()

    @pl.loop(1, N)
    def _(step):
        pl.semaphore_signal(
            barrier, inc=1, device_id=device_of((me + step) % N), device_id_type=MESH
        )

    pl.semaphore_wait(barrier, N - 1)

    def push(src, dst, send_sem, recv_sem, device):
        copy = pltpu.make_async_remote_copy(
            src_ref=src,
            dst_ref=dst,
            send_sem=send_sem,
            recv_sem=recv_sem,
            device_id=device,
            device_id_type=MESH,
        )
        copy.start()
        return copy

    peers = [(a, b) for a in range(G) for b in range(pairs) if (a, b) != (0, 0)]

    def peer_to(a, b):
        return (g + a) % G, ((pair + b) % pairs) * 2 + core

    def peer_from(a, b):
        return ((g + G - a) % G) * R + ((pair + pairs - b) % pairs) * 2

    sibling = (g, t, pair * 2 + other)

    def attn_rows(index):
        return every_attn.at[pl.ds(pl.multiple_of(index * own_rows, own_rows), own_rows), :]

    sends = []
    for n, (a, b) in enumerate(peers):
        to_g, to_r = peer_to(a, b)
        sends.append(
            push(attn_ref, attn_rows(column), attn_send.at[n], attn_recv.at[column], (to_g, t, to_r))
        )
    sends.append(
        push(attn_ref, attn_rows(column), attn_send.at[len(peers)], attn_recv.at[column], sibling)
    )
    every_attn[pl.ds(pl.multiple_of(column * own_rows, own_rows), own_rows), :] = attn_ref[...]

    home_t = column // fold
    home_slot = column % fold

    def skip_rows(slot):
        return skip_block.at[pl.ds(pl.multiple_of(slot * own_rows, own_rows), own_rows), :]

    for j in range(fold):
        dest = t * fold + j
        away = jnp.logical_or(dest != column, home_t != t)
        source = skip_ref.at[:, pl.ds(j * width, width)]

        @pl.when(away)
        def _():
            push(
                source,
                skip_rows(home_slot),
                skip_send.at[j],
                skip_recv.at[home_slot],
                (dest // R, home_t, dest % R),
            )

        @pl.when(jnp.logical_not(away))
        def _():
            pltpu.make_async_copy(source, skip_rows(home_slot), skip_recv.at[home_slot]).start()

    gains[pl.ds(t * fold, fold)] = gain_ref[...]
    for j in range(1, T):
        sends.append(
            push(
                gain_ref,
                gains.at[pl.ds(t * fold, fold)],
                gain_send.at[j],
                gain_recv.at[t],
                (g, (t + j) % T, r),
            )
        )

    for n, (a, b) in enumerate(peers):
        source = peer_from(a, b) + core
        local_wait(attn_rows(source), attn_recv.at[source])
        sends.append(
            push(
                attn_rows(source),
                attn_rows(source),
                attn_send.at[len(peers) + 1 + n],
                attn_recv.at[source],
                sibling,
            )
        )
    local_wait(attn_rows(twin), attn_recv.at[twin])
    for a, b in peers:
        source = peer_from(a, b) + other
        local_wait(attn_rows(source), attn_recv.at[source])

    load_mixing.wait()
    tile = min(256, width)

    @pl.loop(0, width // tile)
    def _(index):
        span = pl.ds(pl.multiple_of(index * tile, tile), tile)
        product = jnp.dot(every_attn[...], mixing[:, span], preferred_element_type=jnp.float32)
        part[:, span] = product
        outgoing[:, span] = product.astype(jnp.bfloat16)

    def block_of(index):
        return pl.ds(pl.multiple_of(index * block_rows, block_rows), block_rows)

    for j in range(1, T):
        to_t = (t + j) % T
        sends.append(
            push(
                outgoing.at[block_of(to_t), :],
                incoming.at[t],
                part_send.at[j],
                part_recv.at[t],
                (g, to_t, r),
            )
        )
    for j in range(fold):
        local_wait(skip_rows(j), skip_recv.at[j])
    total = part[block_of(t), :]
    for j in range(1, T):
        from_t = (t + j) % T
        local_wait(incoming.at[from_t], part_recv.at[from_t])
        total = total + incoming[from_t].astype(jnp.float32)
    hidden = (skip_block[...].astype(jnp.float32) + total).astype(jnp.bfloat16)
    state[column, block_of(t), :] = hidden

    def state_block(col, index):
        return state.at[col, block_of(index), :]

    def spread(index):
        for a, b in peers:
            to_g, to_r = peer_to(a, b)
            push(
                state_block(column, index),
                state_block(column, index),
                plane_send,
                state_recv.at[column, index],
                (to_g, t, to_r),
            )
        push(
            state_block(column, index),
            state_block(column, index),
            plane_send,
            state_recv.at[column, index],
            sibling,
        )

    for j in range(1, T):
        push(
            state_block(column, t),
            state_block(column, t),
            column_send,
            state_recv.at[column, t],
            (g, (t + j) % T, r),
        )
    spread(t)
    for j in range(1, T):
        from_t = (t + j) % T
        local_wait(gains.at[pl.ds(from_t * fold, fold)], gain_recv.at[from_t])
    load_lexicon.wait()
    logits[...] = jnp.zeros_like(logits)
    squares[...] = jnp.zeros_like(squares)

    def head(col):
        wide = state[col].astype(jnp.float32)
        squared = wide * wide
        summed = squares[...]
        for n in range(width // 128):
            summed = summed + squared[:, n * 128 : (n + 1) * 128]
        squares[...] = summed
        scaled = (wide * gains[col]).astype(jnp.bfloat16)
        block = lexicon[pl.ds(pl.multiple_of(col * width, width), width), :]
        logits[...] += jnp.dot(scaled, block, preferred_element_type=jnp.float32)

    for j in range(1, T):
        from_t = (t + j) % T
        local_wait(state_block(column, from_t), state_recv.at[column, from_t])
        spread(from_t)
    head(column)
    for j in range(T):
        from_t = (t + j) % T
        local_wait(state_block(twin, from_t), state_recv.at[twin, from_t])
    head(twin)

    @pl.loop(1, G * pairs)
    def _(step):
        source = peer_from(step // pairs, step % pairs)
        for j in range(T):
            from_t = (t + j) % T
            block = state_block(source + core, from_t)
            local_wait(block, state_recv.at[source + core, from_t])
            push(block, block, pair_send, state_recv.at[source + core, from_t], sibling)
        head(source + core)
        for j in range(T):
            from_t = (t + j) % T
            local_wait(
                state_block(source + other, from_t), state_recv.at[source + other, from_t]
            )
        head(source + other)

    own_span = pl.ds(pl.multiple_of(column * own_rows, own_rows), own_rows)
    for j in range(fold):
        hidden_ref[:, j * width : (j + 1) * width] = state[t * fold + j, own_span, :]

    features = columns * width
    mean_square = jnp.sum(squares[...].T, axis=0, keepdims=True) / features
    row_scale = lax.rsqrt(mean_square + 1e-05) * sharp_ref[...]
    odds = logits[...].T * row_scale
    entry = me * vocab_local + lax.broadcasted_iota(jnp.int32, odds.shape, 0)
    token_part = jnp.sum(jnp.where(entry == chosen_ref[...], odds, 0.0), axis=0, keepdims=True)
    local_top = jnp.max(odds, axis=0, keepdims=True)
    local_total = jnp.sum(jnp.exp(odds - local_top), axis=0, keepdims=True)
    stats[me] = jnp.concatenate(
        [local_top, local_total, token_part, jnp.zeros((5, rows), jnp.float32)], axis=0
    )

    def share(buffer, sems):
        @pl.loop(1, N)
        def _(step):
            push(
                buffer.at[me],
                buffer.at[me],
                sems.at[0],
                sems.at[1],
                device_of((me + step) % N),
            )

        local_wait(buffer.at[pl.ds(0, N - 1)], sems.at[1])

    share(stats, stats_sems)
    tops = stats[:, 0, :]
    top = jnp.max(tops, axis=0, keepdims=True)
    sum_exp = jnp.sum(stats[:, 1, :] * jnp.exp(tops - top), axis=0, keepdims=True)
    token_logit = jnp.sum(stats[:, 2, :], axis=0, keepdims=True)
    lognorm = top + jnp.log(sum_exp)
    mu = mu_ref[...]
    logp = odds - lognorm
    margin = cut_slope * (mu + logp / math.log(2.0))
    tail = jnp.exp(-jnp.abs(margin))
    weight = jnp.where(margin >= 0.0, 1.0, tail) / (1.0 + tail)
    kept_local = jnp.sum(jnp.exp(logp) * weight, axis=0, keepdims=True)
    kept_parts[me] = jnp.broadcast_to(kept_local, (8, rows))
    share(kept_parts, kept_sems)
    kept = jnp.sum(kept_parts[:, 0, :], axis=0, keepdims=True)
    token_logp = token_logit - lognorm
    token_margin = cut_slope * (mu + token_logp / math.log(2.0))
    token_logw = (
        token_logp
        + jnp.minimum(token_margin, 0.0)
        - jnp.log1p(jnp.exp(-jnp.abs(token_margin)))
    )
    surprise = -(token_logw - jnp.log(kept)) / math.log(2.0)
    surprise_ref[...] = surprise
    targets_ref[...] = mu - 0.1 * (surprise - 5.0)

    for copy in sends:
        copy.wait_send()
    for j in range(fold):
        away = jnp.logical_or(t * fold + j != column, home_t != t)

        @pl.when(away)
        def _():
            local_wait(skip_ref.at[:, pl.ds(j * width, width)], skip_send.at[j])

    local_wait(state.at[0, pl.ds(0, (T - 1) * block_rows), :], column_send)
    local_wait(state.at[pl.ds(0, len(peers) + 1)], plane_send)
    local_wait(state.at[pl.ds(0, len(peers))], pair_send)
    local_wait(stats.at[pl.ds(0, N - 1)], stats_sems.at[0])
    local_wait(kept_parts.at[pl.ds(0, N - 1)], kept_sems.at[0])


def tail(sizes, attn, mixing, skip, gain, lexicon, sharp, mu, chosen):
    G, T, R = sizes
    N = G * T * R
    columns = G * R
    fold = columns // T
    own_rows = attn.shape[0]
    rows = own_rows * columns
    block_rows = rows // T
    width = mixing.shape[1]
    depth = mixing.shape[0]
    features, vocab_local = lexicon.shape
    peers = columns // 2 - 1
    vmem = pl.BlockSpec(memory_space=pltpu.VMEM)
    hbm = pl.BlockSpec(memory_space=pl.ANY)
    dma = pltpu.SemaphoreType.DMA
    hidden, targets, surprise = pl.pallas_call(
        functools.partial(tail_kernel, sizes),
        out_shape=(
            jax.ShapeDtypeStruct(skip.shape, jnp.bfloat16),
            jax.ShapeDtypeStruct((1, rows), jnp.float32),
            jax.ShapeDtypeStruct((1, rows), jnp.float32),
        ),
        in_specs=[vmem, hbm, vmem, vmem, hbm, vmem, vmem, vmem],
        out_specs=(vmem, vmem, vmem),
        scratch_shapes=[
            pltpu.VMEM(mixing.shape, jnp.bfloat16),
            pltpu.VMEM(lexicon.shape, jnp.bfloat16),
            pltpu.VMEM((rows, depth), jnp.bfloat16),
            pltpu.VMEM((rows, width), jnp.float32),
            pltpu.VMEM((rows, width), jnp.bfloat16),
            pltpu.VMEM((T, block_rows, width), jnp.bfloat16),
            pltpu.VMEM((block_rows, width), jnp.bfloat16),
            pltpu.VMEM((columns, 1, width), jnp.float32),
            pltpu.VMEM((columns, rows, width), jnp.bfloat16),
            pltpu.VMEM((rows, vocab_local), jnp.float32),
            pltpu.VMEM((rows, 128), jnp.float32),
            pltpu.VMEM((N, 8, rows), jnp.float32),
            pltpu.VMEM((N, 8, rows), jnp.float32),
            dma((2,)),
            dma((2 * peers + 1,)),
            dma((columns,)),
            dma((fold,)),
            dma((fold,)),
            dma((T,)),
            dma((T,)),
            dma((T,)),
            dma((T,)),
            dma,
            dma,
            dma,
            dma((columns, T)),
            dma((2,)),
            dma((2,)),
        ],
        compiler_params=pltpu.CompilerParams(
            collective_id=0, has_side_effects=True, vmem_limit_bytes=56 * 2**20
        ),
    )(
        attn,
        mixing,
        skip,
        gain.astype(jnp.float32).reshape(fold, 1, width),
        lexicon,
        sharp.reshape(1, rows),
        mu.reshape(1, rows),
        chosen.reshape(1, rows),
    )
    return hidden, targets.reshape(rows), surprise.reshape(rows)


def solution(mesh):
    sizes = tuple(mesh.shape[a] for a in axes)

    def shards(
        probe_vectors,
        stored_lookup_vectors,
        stored_content_vectors,
        fresh_lookup_vector,
        fresh_content_vector,
        history_counts,
        mixing_matrix,
        skip_stream,
        closing_multiplier,
        lexicon_matrix,
        sharpening_factor,
        desired_perplexity,
        chosen_symbols,
    ):
        attn = attend(
            probe_vectors,
            stored_lookup_vectors,
            stored_content_vectors,
            fresh_lookup_vector,
            fresh_content_vector,
            history_counts,
        )
        return tail(
            sizes,
            attn,
            mixing_matrix,
            skip_stream,
            closing_multiplier,
            lexicon_matrix,
            sharpening_factor,
            desired_perplexity,
            chosen_symbols,
        )

    placed = (
        P(("group", "rep"), "tensor", None),
        P(("group", "rep"), "tensor", None, None),
        P(("group", "rep"), "tensor", None, None),
        P(("group", "rep"), "tensor", None),
        P(("group", "rep"), "tensor", None),
        P(("group", "rep")),
        P("tensor", ("group", "rep")),
        P(("group", "rep"), "tensor"),
        P("tensor"),
        P(None, ("group", "tensor", "rep")),
        P(),
        P(),
        P(),
    )
    return jax.shard_map(
        shards,
        mesh=mesh,
        in_specs=placed,
        out_specs=(P(("group", "rep"), "tensor"), P(), P()),
        check_vma=False,
    )
```

time: 246 us -> 67.9 us (0.28)
  blocking collectives: 166 us -> 0 us
  Pallas kernels: 0 us -> 55.9 us
  waiting for transfers between devices: 49.6 us -> 0 us
  between operations: 14.2 us -> 0.73 us
  matrix products: 11.3 us -> 4.74 us
  local copies, waits for them, and re-layouts: 0.91 us -> 4.45 us
    psum x3 -> x0, blocking collectives: 88.9 us -> none  [the longest x1 41 us: shards(): lax.psum((local_total, token_part), ('group', 'tensor', 'rep'))]
    pallas_call x0 -> x1, Pallas kernels: none -> 55.9 us  [tail(): pl.pallas_call(functools.partial(tail_kernel, sizes), out_shape=(jax.Shap...]
    pmax x1 -> x0, blocking collectives: 39.4 us -> none  [shards(): lax.pmax(jnp.max(unnormalized_odds, axis=1), ('group', 'tensor', 'rep'))]
    all_gather x1 -> x0, waiting for transfers between devices: 27.5 us -> none  [shards(): lax.all_gather(features, ('group', 'rep'), axis=0, tiled=True)]
    all_gather x2 -> x0, blocking collectives: 26 us -> none  [the longest x1 14.5 us: shards(): features = lax.all_gather(rescaled_stream, 'tensor', axis=1, tiled=True)]
    reduce_scatter x1 -> x0, waiting for transfers between devices: 22 us -> none  [shards(): summed = lax.psum_scatter(terms, 'tensor', scatter_dimension=1, tiled=True)]
    all_to_all x1 -> x0, blocking collectives: 11.5 us -> none  [shards(): lax.all_to_all(partial_cols, ('group', 'rep'), split_axis=0, concat_axis=...]
    dot_general x2 -> x0, matrix products: 6.08 us -> none  [the longest x1 5.36 us: shards(): jnp.dot(lax.all_gather(features, ('group', 'rep'), axis=0, tiled=True), l...]
  transfers between devices with their start and end apart: 2 -> 0, of which waited for: 2 -> 0; matrix products, arithmetic and copies ran while one was open for 0% -> 0% of each run, Pallas kernels for 0% -> 0%
where the time goes in v1:
time: 67.9 us; the launch traced here: 67.7 us
  Pallas kernels  55.9 us (82%)
  matrix products  4.74 us (7%)
  local copies, waits for them, and re-layouts  4.45 us (7%)
  other arithmetic  1.8 us (3%)
  between operations  0.73 us (1%)
    pallas_call x1, Pallas kernels, tail(): pl.pallas_call(functools.partial(tail_kernel, sizes), out_shape=(jax.Shap...  55.9 us
    unnamed x14, local copies, waits for them, and re-layouts  4.45 us
    dot_general x1, matrix products, attend(): jnp.einsum('bkgd,bkld->bkgl', grouped_query_rows, stored_lookup_vectors,...  3.87 us

profile of v1, /device:TPU:0, one launch (start us, length us, event | category | flops | bytes accessed | tf_op | source)
XLA Modules:
  0.0 67.7 jit_solution(7323554913248260974)
XLA Ops:
  0.6 0.0 copy-start
  0.6 0.0 copy-start.4
  0.7 0.0 copy-start.1
  0.7 0.0 copy-start.3
  0.7 0.9 %iota_compare_fusion = pred[16,512]{1,0:T(8,128)(4,1)S(1)} fusion(s32[16]{0:T(128)} %param.18), kind=kLoop, calls=%fused_computation.15 | loop fusion | flops 8192 | bytes 8256 | tf_op jit(solution)/shard_map/lt | solution.py:46
  1.6 0.0 copy-done
  1.6 3.9 %select_reduce_fusion = (f32[16,2,8]{2,1,0:T(2,128)S(1)}, f32[16,2,8,512]{3,2,1,0:T(8,128)S(1)}) fusion(pred[16,512]{1,0:T(8,128)(4,1)S(1)} %iota_compare_fusion, bf16[16,2,512,128]{3,2,1,0:T(8,128)(2,1)} %param.14, bf16[16,16,128]{2,1,0:T(8,128)(2,1)S(1)} %copy-done), kind=kOutput, calls=%fused_computation.5 | convolution fusion | flops 33947392 | bytes 4793344 | tf_op jit(solution)/shard_map/bkgd,bkld->bkgl/dot_general | solution.py:37
  5.4 0.0 copy-start.2
  5.5 0.0 copy-done.4
  5.5 0.1 fusion.8
  5.6 0.3 fusion.2
  5.9 0.0 copy-done.1
  6.0 0.0 copy-done.3
  6.0 0.7 %fusion.1 = bf16[16,2,8,128]{3,2,1,0:T(8,128)(2,1)S(1)} fusion(bf16[16,2,512,128]{3,2,1,0:T(8,128)(2,1)S(1)} %copy-done.3, f32[16,2,8,512]{3,2,1,0:T(8,128)S(1)} %get-tuple-element.12, f32[16,2,8]{2,1,0:T(2,128)S(1)} %multiply_maximum_fusion, pred[16,512]{1,0:T(8,128)(4,1)S(1)} %iota_compare_fusion, f32[16,2,8]{2,1,0:T(2,128)S(1)} %get-tuple-element.10, ...), kind=kOutput, calls=%fused_computation.3 | convolution fusion | flops 34078720 | bytes 4811776 | tf_op jit(solution)/shard_map/bkgl,bkld->bkgd/dot_general | solution.py:50
  6.7 0.7 copy.22
  7.4 0.0 copy-done.2
  7.4 0.6 reshape.62
  8.0 55.9 %shard_map.148 = (bf16[16,2048]{1,0:T(8,128)(2,1)}, f32[1,128]{1,0:T(1,128)}, f32[1,128]{1,0:T(1,128)}) custom-call(bf16[16,2048]{1,0:T(8,128)(2,1)} %bitcast.23, bf16[2048,1024]{1,0:T(8,128)(2,1)} %mixing_hbm.1, bf16[16,2048]{1,0:T(8,128)(2,1)} %skip_ref.1, f32[2,1,1024]{2,1,0:T(1,128)} %bitcast.27, bf16[8192,512]{1,0:T(8,128)(2,1)} %lexicon_hbm.1, ...), custom_call_target="tpu_custom_call" | custom-call | tf_op jit(solution)/shard_map/pallas_call | solution.py:436
  63.9 1.5 %copy.26 = bf16[16,2048]{1,0:T(8,128)(2,1)} copy(bf16[16,2048]{1,0:T(8,128)(2,1)} %get-tuple-element.16) | data formatting | bytes 131072
  65.4 1.1 %copy.27 = f32[128]{0:T(128)} copy(f32[128]{0:T(128)} %bitcast.33) | data formatting | bytes 1024
  66.5 1.2 %copy.28 = f32[128]{0:T(128)} copy(f32[128]{0:T(128)} %bitcast.32) | data formatting | bytes 1024
  (3 shorter events, 0.1 us)
Async XLA Ops:
  0.6 0.9 %copy-start = (bf16[16,16,128]{2,1,0:T(8,128)(2,1)S(1)}, bf16[16,16,128]{2,1,0:T(8,128)(2,1)}, u32[]{:S(2)}) copy-start(bf16[16,16,128]{2,1,0:T(8,128)(2,1)} %param.13) | copy-start | bytes 196612
  0.6 4.8 %copy-start.4 = (bf16[16,2,128]{2,1,0:T(2,128)(2,1)S(1)}, bf16[16,2,128]{2,1,0:T(2,128)(2,1)}, u32[]{:S(2)}) copy-start(bf16[16,2,128]{2,1,0:T(2,128)(2,1)} %param.16) | copy-start | bytes 24580
  0.7 5.3 %copy-start.1 = (bf16[16,2,128]{2,1,0:T(2,128)(2,1)S(1)}, bf16[16,2,128]{2,1,0:T(2,128)(2,1)}, u32[]{:S(2)}) copy-start(bf16[16,2,128]{2,1,0:T(2,128)(2,1)} %param.17) | copy-start | bytes 24580
  0.7 5.3 %copy-start.3 = (bf16[16,2,512,128]{3,2,1,0:T(8,128)(2,1)S(1)}, bf16[16,2,512,128]{3,2,1,0:T(8,128)(2,1)}, u32[]{:S(2)}) copy-start(bf16[16,2,512,128]{3,2,1,0:T(8,128)(2,1)} %param.15) | copy-start | bytes 12582916
  5.4 1.9 %copy-start.2 = (bf16[2048]{0:T(1024)(128)(2,1)S(1)}, bf16[2048]{0:T(1024)(128)(2,1)}, u32[]{:S(2)}) copy-start(bf16[2048]{0:T(1024)(128)(2,1)} %param.21) | copy-start | bytes 12292

commit v2 on v1

--- a/solution.py
+++ b/solution.py
@@ -12,58 +12,6 @@
 MESH = pl.DeviceIdType.MESH
 
 
-def attend(
-    probe_vectors,
-    stored_lookup_vectors,
-    stored_content_vectors,
-    fresh_lookup_vector,
-    fresh_content_vector,
-    history_counts,
-):
-    rows, kv_local, cache_len, head_dim = stored_lookup_vectors.shape
-    heads_local = probe_vectors.shape[1]
-    grouped_query_rows = probe_vectors.reshape(rows, kv_local, heads_local // kv_local, head_dim)
-    score_scale = 1.0 / math.sqrt(head_dim)
-    self_entry = (
-        jnp.einsum(
-            "mjqo,mjo->mjq",
-            grouped_query_rows,
-            fresh_lookup_vector,
-            preferred_element_type=jnp.float32,
-        )
-        * score_scale
-    )
-    scores = (
-        jnp.einsum(
-            "bkgd,bkld->bkgl",
-            grouped_query_rows,
-            stored_lookup_vectors,
-            preferred_element_type=jnp.float32,
-        )
-        * score_scale
-    )
-    position = lax.broadcasted_iota(jnp.int32, (1, 1, 1, cache_len), 3)
-    live = position < history_counts[:, None, None, None]
-    top = jnp.maximum(jnp.max(jnp.where(live, scores, -1e30), axis=3), self_entry)
-    expo = jnp.where(live, jnp.exp(scores - top[..., None]), 0.0)
-    total = jnp.sum(expo, axis=3)
-    accum = jnp.einsum(
-        "bkgl,bkld->bkgd",
-        expo.astype(jnp.bfloat16),
-        stored_content_vectors,
-        preferred_element_type=jnp.float32,
-    )
-    own_expo = jnp.exp(self_entry - top)
-    total = total + own_expo
-    accum = accum + jnp.einsum(
-        "vct,vcn->vctn",
-        own_expo.astype(jnp.bfloat16),
-        fresh_content_vector,
-        preferred_element_type=jnp.float32,
-    )
-    return (accum / total[..., None]).reshape(rows, heads_local * head_dim).astype(jnp.bfloat16)
-
-
 axes = ("group", "tensor", "rep")
 
 
@@ -73,7 +21,12 @@
 
 def tail_kernel(
     sizes,
-    attn_ref,
+    probe_ref,
+    keys_hbm,
+    values_hbm,
+    own_key_ref,
+    own_value_ref,
+    counts_ref,
     mixing_hbm,
     skip_ref,
     gain_ref,
@@ -84,19 +37,24 @@
     hidden_ref,
     targets_ref,
     surprise_ref,
+    keys,
+    values,
+    row_attn,
+    attn_ref,
     mixing,
     lexicon,
     every_attn,
     part,
-    outgoing,
     incoming,
     skip_block,
-    gains,
+    gain_block,
+    hidden_block,
+    square_sums,
     state,
     logits,
-    squares,
     stats,
     kept_parts,
+    cache_sems,
     load_sems,
     attn_send,
     attn_recv,
@@ -104,6 +62,9 @@
     skip_recv,
     gain_send,
     gain_recv,
+    back_send,
+    back_recv,
+    square_sems,
     part_send,
     part_recv,
     column_send,
@@ -118,7 +79,9 @@
     columns = G * R
     fold = columns // T
     pairs = R // 2
-    own_rows = attn_ref.shape[0]
+    own_rows, heads, head_dim = probe_ref.shape
+    kv_heads = own_key_ref.shape[1]
+    cache_len = keys.shape[2]
     rows = every_attn.shape[0]
     block_rows = rows // T
     width = mixing.shape[1]
@@ -133,19 +96,105 @@
 
     load_mixing = pltpu.make_async_copy(mixing_hbm, mixing, load_sems.at[0])
     load_lexicon = pltpu.make_async_copy(lexicon_hbm, lexicon, load_sems.at[1])
+    group_rows = own_rows // cache_sems.shape[1]
+
+    def cache_loads(index):
+        span = pl.ds(index * group_rows, group_rows)
+        return [
+            pltpu.make_async_copy(source.at[span], dest.at[span], cache_sems.at[n, index])
+            for n, (source, dest) in enumerate(((keys_hbm, keys), (values_hbm, values)))
+        ]
+
+    @pl.loop(0, own_rows // group_rows)
+    def _(index):
+        for load in cache_loads(index):
+            load.start()
+
     load_mixing.start()
     load_lexicon.start()
 
-    def device_of(index):
-        return (index // (T * R), (index // R) % T, index % R)
+    def wrap(position, size):
+        return jnp.where(position >= size, position - size, position)
+
+    def every_other(visit):
+        for a in range(G):
+            to_g = wrap(g + a, G)
+
+            @pl.loop(1 if a == 0 else 0, T)
+            def _(b):
+                to_t = wrap(t + b, T)
+                for d in range(R):
+                    visit((to_g, to_t, wrap(r + d, R)))
+
+        for d in range(1, R):
+            visit((g, t, wrap(r + d, R)))
 
     barrier = pltpu.get_barrier_semaphore()
-
-    @pl.loop(1, N)
-    def _(step):
-        pl.semaphore_signal(
-            barrier, inc=1, device_id=device_of((me + step) % N), device_id_type=MESH
-        )
+    every_other(
+        lambda device: pl.semaphore_signal(
+            barrier, inc=1, device_id=device, device_id_type=MESH
+        )
+    )
+
+    score_scale = 1.0 / math.sqrt(head_dim)
+    share_of = heads // kv_heads
+    position = lax.broadcasted_iota(jnp.int32, (heads, cache_len), 1)
+
+    def spread_heads(pair_rows):
+        wide = pair_rows.astype(jnp.float32)
+        return jnp.concatenate(
+            [jnp.broadcast_to(wide[k : k + 1], (share_of, head_dim)) for k in range(kv_heads)],
+            axis=0,
+        )
+
+    def per_head(products):
+        return jnp.concatenate(
+            [products[k][k * share_of : (k + 1) * share_of] for k in range(kv_heads)], axis=0
+        )
+
+    def attend(row):
+        query = probe_ref[row]
+        scores = score_scale * per_head(
+            [
+                lax.dot_general(
+                    query,
+                    keys[row, k],
+                    (((1,), (1,)), ((), ())),
+                    preferred_element_type=jnp.float32,
+                )
+                for k in range(kv_heads)
+            ]
+        )
+        own = score_scale * jnp.sum(
+            query.astype(jnp.float32) * spread_heads(own_key_ref[row]), axis=1, keepdims=True
+        )
+        live = position < counts_ref[row]
+        peak = jnp.maximum(
+            jnp.max(jnp.where(live, scores, -1e30), axis=1, keepdims=True), own
+        )
+        expo = jnp.where(live, jnp.exp(scores - peak), 0.0)
+        own_expo = jnp.exp(own - peak)
+        total = jnp.sum(expo, axis=1, keepdims=True) + own_expo
+        weights = expo.astype(jnp.bfloat16)
+        accum = per_head(
+            [
+                jnp.dot(weights, values[row, k], preferred_element_type=jnp.float32)
+                for k in range(kv_heads)
+            ]
+        )
+        own_weight = own_expo.astype(jnp.bfloat16).astype(jnp.float32)
+        accum = accum + own_weight * spread_heads(own_value_ref[row])
+        row_attn[row] = accum / total
+
+    @pl.loop(0, own_rows // group_rows)
+    def _(index):
+        for load in cache_loads(index):
+            load.wait()
+        for n in range(group_rows):
+            attend(index * group_rows + n)
+
+    for h in range(heads):
+        attn_ref[:, h * head_dim : (h + 1) * head_dim] = row_attn[:, h, :].astype(jnp.bfloat16)
 
     pl.semaphore_wait(barrier, N - 1)
 
@@ -205,22 +254,20 @@
                 skip_recv.at[home_slot],
                 (dest // R, home_t, dest % R),
             )
+            push(
+                gain_ref.at[j],
+                gain_block.at[home_slot],
+                gain_send.at[j],
+                gain_recv.at[home_slot],
+                (dest // R, home_t, dest % R),
+            )
 
         @pl.when(jnp.logical_not(away))
         def _():
             pltpu.make_async_copy(source, skip_rows(home_slot), skip_recv.at[home_slot]).start()
-
-    gains[pl.ds(t * fold, fold)] = gain_ref[...]
-    for j in range(1, T):
-        sends.append(
-            push(
-                gain_ref,
-                gains.at[pl.ds(t * fold, fold)],
-                gain_send.at[j],
-                gain_recv.at[t],
-                (g, (t + j) % T, r),
-            )
-        )
+            pltpu.make_async_copy(
+                gain_ref.at[j], gain_block.at[home_slot], gain_recv.at[home_slot]
+            ).start()
 
     for n, (a, b) in enumerate(peers):
         source = peer_from(a, b) + core
@@ -245,9 +292,9 @@
     @pl.loop(0, width // tile)
     def _(index):
         span = pl.ds(pl.multiple_of(index * tile, tile), tile)
-        product = jnp.dot(every_attn[...], mixing[:, span], preferred_element_type=jnp.float32)
-        part[:, span] = product
-        outgoing[:, span] = product.astype(jnp.bfloat16)
+        part[:, span] = jnp.dot(
+            every_attn[...], mixing[:, span], preferred_element_type=jnp.float32
+        )
 
     def block_of(index):
         return pl.ds(pl.multiple_of(index * block_rows, block_rows), block_rows)
@@ -256,7 +303,7 @@
         to_t = (t + j) % T
         sends.append(
             push(
-                outgoing.at[block_of(to_t), :],
+                part.at[block_of(to_t), :],
                 incoming.at[t],
                 part_send.at[j],
                 part_recv.at[t],
@@ -265,13 +312,65 @@
         )
     for j in range(fold):
         local_wait(skip_rows(j), skip_recv.at[j])
+        local_wait(gain_block.at[j], gain_recv.at[j])
     total = part[block_of(t), :]
     for j in range(1, T):
         from_t = (t + j) % T
         local_wait(incoming.at[from_t], part_recv.at[from_t])
-        total = total + incoming[from_t].astype(jnp.float32)
+        total = total + incoming[from_t]
     hidden = (skip_block[...].astype(jnp.float32) + total).astype(jnp.bfloat16)
-    state[column, block_of(t), :] = hidden
+    hidden_block[...] = hidden
+
+    def back_target(j):
+        owner = t * fold + j
+        return owner, column // fold, column % fold
+
+    def hidden_slot(slot):
+        return hidden_ref.at[:, pl.ds(pl.multiple_of(slot * width, width), width)]
+
+    wide = hidden.astype(jnp.float32)
+    row_squares = jnp.sum(wide * wide, axis=1, keepdims=True)
+    diagonal = lax.broadcasted_iota(jnp.int32, (block_rows, 128), 1) == (
+        lax.broadcasted_iota(jnp.int32, (block_rows, 128), 0)
+    )
+    square_sums[column] = jnp.sum(
+        jnp.where(diagonal, row_squares, 0.0), axis=0, keepdims=True
+    )
+    for a in range(G):
+        for d in range(R):
+            if (a, d) != (0, 0):
+                push(
+                    square_sums.at[column],
+                    square_sums.at[column],
+                    square_sems.at[0],
+                    square_sems.at[1],
+                    (wrap(g + a, G), t, wrap(r + d, R)),
+                )
+    for j in range(fold):
+        owner, at_t, slot = back_target(j)
+        away = jnp.logical_or(owner != column, at_t != t)
+        source = hidden_block.at[pl.ds(j * own_rows, own_rows), :]
+
+        @pl.when(away)
+        def _():
+            push(
+                source,
+                hidden_slot(slot),
+                back_send.at[j],
+                back_recv.at[slot],
+                (owner // R, at_t, owner % R),
+            )
+
+        @pl.when(jnp.logical_not(away))
+        def _():
+            pltpu.make_async_copy(source, hidden_slot(slot), back_recv.at[slot]).start()
+
+    local_wait(square_sums.at[pl.ds(0, columns - 1)], square_sems.at[1])
+    mean_square = jnp.sum(square_sums[...], axis=0) / (columns * width)
+    scale = lax.rsqrt(
+        jnp.sum(jnp.where(diagonal, mean_square, 0.0), axis=1, keepdims=True) + 1e-05
+    )
+    state[column, block_of(t), :] = (wide * scale * gain_block[0]).astype(jnp.bfloat16)
 
     def state_block(col, index):
         return state.at[col, block_of(index), :]
@@ -303,23 +402,12 @@
             (g, (t + j) % T, r),
         )
     spread(t)
-    for j in range(1, T):
-        from_t = (t + j) % T
-        local_wait(gains.at[pl.ds(from_t * fold, fold)], gain_recv.at[from_t])
     load_lexicon.wait()
     logits[...] = jnp.zeros_like(logits)
-    squares[...] = jnp.zeros_like(squares)
 
     def head(col):
-        wide = state[col].astype(jnp.float32)
-        squared = wide * wide
-        summed = squares[...]
-        for n in range(width // 128):
-            summed = summed + squared[:, n * 128 : (n + 1) * 128]
-        squares[...] = summed
-        scaled = (wide * gains[col]).astype(jnp.bfloat16)
         block = lexicon[pl.ds(pl.multiple_of(col * width, width), width), :]
-        logits[...] += jnp.dot(scaled, block, preferred_element_type=jnp.float32)
+        logits[...] += jnp.dot(state[col], block, preferred_element_type=jnp.float32)
 
     for j in range(1, T):
         from_t = (t + j) % T
@@ -347,14 +435,7 @@
             )
         head(source + other)
 
-    own_span = pl.ds(pl.multiple_of(column * own_rows, own_rows), own_rows)
-    for j in range(fold):
-        hidden_ref[:, j * width : (j + 1) * width] = state[t * fold + j, own_span, :]
-
-    features = columns * width
-    mean_square = jnp.sum(squares[...].T, axis=0, keepdims=True) / features
-    row_scale = lax.rsqrt(mean_square + 1e-05) * sharp_ref[...]
-    odds = logits[...].T * row_scale
+    odds = logits[...].T * sharp_ref[...]
     entry = me * vocab_local + lax.broadcasted_iota(jnp.int32, odds.shape, 0)
     token_part = jnp.sum(jnp.where(entry == chosen_ref[...], odds, 0.0), axis=0, keepdims=True)
     local_top = jnp.max(odds, axis=0, keepdims=True)
@@ -364,16 +445,11 @@
     )
 
     def share(buffer, sems):
-        @pl.loop(1, N)
-        def _(step):
-            push(
-                buffer.at[me],
-                buffer.at[me],
-                sems.at[0],
-                sems.at[1],
-                device_of((me + step) % N),
-            )
-
+        every_other(
+            lambda device: push(
+                buffer.at[me], buffer.at[me], sems.at[0], sems.at[1], device
+            )
+        )
         local_wait(buffer.at[pl.ds(0, N - 1)], sems.at[1])
 
     share(stats, stats_sems)
@@ -388,9 +464,9 @@
     tail = jnp.exp(-jnp.abs(margin))
     weight = jnp.where(margin >= 0.0, 1.0, tail) / (1.0 + tail)
     kept_local = jnp.sum(jnp.exp(logp) * weight, axis=0, keepdims=True)
-    kept_parts[me] = jnp.broadcast_to(kept_local, (8, rows))
+    kept_parts[me] = kept_local
     share(kept_parts, kept_sems)
-    kept = jnp.sum(kept_parts[:, 0, :], axis=0, keepdims=True)
+    kept = jnp.sum(kept_parts[...], axis=0)
     token_logp = token_logit - lognorm
     token_margin = cut_slope * (mu + token_logp / math.log(2.0))
     token_logw = (
@@ -410,7 +486,17 @@
         @pl.when(away)
         def _():
             local_wait(skip_ref.at[:, pl.ds(j * width, width)], skip_send.at[j])
-
+            local_wait(gain_ref.at[j], gain_send.at[j])
+
+        owner, at_t, slot = back_target(j)
+
+        @pl.when(jnp.logical_or(owner != column, at_t != t))
+        def _():
+            local_wait(hidden_block.at[pl.ds(j * own_rows, own_rows), :], back_send.at[j])
+
+        local_wait(hidden_slot(j), back_recv.at[j])
+
+    local_wait(square_sums.at[pl.ds(0, columns - 1)], square_sems.at[0])
     local_wait(state.at[0, pl.ds(0, (T - 1) * block_rows), :], column_send)
     local_wait(state.at[pl.ds(0, len(peers) + 1)], plane_send)
     local_wait(state.at[pl.ds(0, len(peers))], pair_send)
@@ -418,12 +504,19 @@
     local_wait(kept_parts.at[pl.ds(0, N - 1)], kept_sems.at[0])
 
 
-def tail(sizes, attn, mixing, skip, gain, lexicon, sharp, mu, chosen):
+def finish_kernel(hidden_in, targets_in, surprise_in, hidden_ref, targets_ref, surprise_ref):
+    hidden_ref[...] = hidden_in[...]
+    targets_ref[...] = targets_in[...]
+    surprise_ref[...] = surprise_in[...]
+
+
+def tail(sizes, probe, keys, values, own_key, own_value, counts, mixing, skip, gain, lexicon, sharp, mu, chosen):
     G, T, R = sizes
     N = G * T * R
     columns = G * R
     fold = columns // T
-    own_rows = attn.shape[0]
+    own_rows, heads, head_dim = probe.shape
+    load_groups = math.gcd(own_rows, 4)
     rows = own_rows * columns
     block_rows = rows // T
     width = mixing.shape[1]
@@ -433,36 +526,45 @@
     vmem = pl.BlockSpec(memory_space=pltpu.VMEM)
     hbm = pl.BlockSpec(memory_space=pl.ANY)
     dma = pltpu.SemaphoreType.DMA
-    hidden, targets, surprise = pl.pallas_call(
+    out_shape = (
+        jax.ShapeDtypeStruct(skip.shape, jnp.bfloat16),
+        jax.ShapeDtypeStruct((1, rows), jnp.float32),
+        jax.ShapeDtypeStruct((1, rows), jnp.float32),
+    )
+    results = pl.pallas_call(
         functools.partial(tail_kernel, sizes),
-        out_shape=(
-            jax.ShapeDtypeStruct(skip.shape, jnp.bfloat16),
-            jax.ShapeDtypeStruct((1, rows), jnp.float32),
-            jax.ShapeDtypeStruct((1, rows), jnp.float32),
-        ),
-        in_specs=[vmem, hbm, vmem, vmem, hbm, vmem, vmem, vmem],
+        out_shape=out_shape,
+        in_specs=[vmem, hbm, hbm, vmem, vmem, pl.BlockSpec(memory_space=pltpu.SMEM), hbm, vmem, vmem, hbm, vmem, vmem, vmem],
         out_specs=(vmem, vmem, vmem),
         scratch_shapes=[
+            pltpu.VMEM(keys.shape, jnp.bfloat16),
+            pltpu.VMEM(values.shape, jnp.bfloat16),
+            pltpu.VMEM((own_rows, heads, head_dim), jnp.float32),
+            pltpu.VMEM((own_rows, depth), jnp.bfloat16),
             pltpu.VMEM(mixing.shape, jnp.bfloat16),
             pltpu.VMEM(lexicon.shape, jnp.bfloat16),
             pltpu.VMEM((rows, depth), jnp.bfloat16),
             pltpu.VMEM((rows, width), jnp.float32),
-            pltpu.VMEM((rows, width), jnp.bfloat16),
-            pltpu.VMEM((T, block_rows, width), jnp.bfloat16),
+            pltpu.VMEM((T, block_rows, width), jnp.float32),
             pltpu.VMEM((block_rows, width), jnp.bfloat16),
-            pltpu.VMEM((columns, 1, width), jnp.float32),
+            pltpu.VMEM((fold, 1, width), jnp.float32),
+            pltpu.VMEM((block_rows, width), jnp.bfloat16),
+            pltpu.VMEM((columns, 1, 128), jnp.float32),
             pltpu.VMEM((columns, rows, width), jnp.bfloat16),
             pltpu.VMEM((rows, vocab_local), jnp.float32),
-            pltpu.VMEM((rows, 128), jnp.float32),
             pltpu.VMEM((N, 8, rows), jnp.float32),
-            pltpu.VMEM((N, 8, rows), jnp.float32),
+            pltpu.VMEM((N, 1, rows), jnp.float32),
+            dma((2, load_groups)),
             dma((2,)),
             dma((2 * peers + 1,)),
             dma((columns,)),
             dma((fold,)),
             dma((fold,)),
-            dma((T,)),
-            dma((T,)),
+            dma((fold,)),
+            dma((fold,)),
+            dma((fold,)),
+            dma((fold,)),
+            dma((2,)),
             dma((T,)),
             dma((T,)),
             dma,
@@ -476,7 +578,12 @@
             collective_id=0, has_side_effects=True, vmem_limit_bytes=56 * 2**20
         ),
     )(
-        attn,
+        probe,
+        keys,
+        values,
+        own_key,
+        own_value,
+        counts,
         mixing,
         skip,
         gain.astype(jnp.float32).reshape(fold, 1, width),
@@ -485,6 +592,9 @@
         mu.reshape(1, rows),
         chosen.reshape(1, rows),
     )
+    hidden, targets, surprise = pl.pallas_call(
+        finish_kernel, out_shape=out_shape, in_specs=[vmem] * 3, out_specs=(vmem,) * 3
+    )(*results)
     return hidden, targets.reshape(rows), surprise.reshape(rows)
 
 
@@ -506,17 +616,14 @@
         desired_perplexity,
         chosen_symbols,
     ):
-        attn = attend(
+        return tail(
+            sizes,
             probe_vectors,
             stored_lookup_vectors,
             stored_content_vectors,
             fresh_lookup_vector,
             fresh_content_vector,
             history_counts,
-        )
-        return tail(
-            sizes,
-            attn,
             mixing_matrix,
             skip_stream,
             closing_multiplier,

time: 67.9 us -> 73.5 us (1.082)
  Pallas kernels: 55.9 us -> 71.3 us
  matrix products: 4.74 us -> 0 us
  local copies, waits for them, and re-layouts: 4.45 us -> 0 us
    pallas_call x1 -> x2, Pallas kernels: 55.9 us -> 71.3 us  [the longest x1 69.8 us: tail(): pl.pallas_call(functools.partial(tail_kernel, sizes), out_shape=out_shape...]
    dot_general x3 -> x0, matrix products: 4.74 us -> none  [the longest x1 3.87 us: attend(): jnp.einsum('bkgd,bkld->bkgl', grouped_query_rows, stored_lookup_vectors,...]
    unnamed x14 -> x0, local copies, waits for them, and re-layouts: 4.45 us -> none
    lt x1 -> x0, other arithmetic: 0.88 us -> none  [attend(): live = position < history_counts[:, None, None, None]]
where the time goes in v2:
time: 73.5 us; the launch traced here: 73.2 us
  Pallas kernels  71.3 us (97%)
  other arithmetic  1.29 us (2%)
    pallas_call x1, Pallas kernels, tail(): pl.pallas_call(functools.partial(tail_kernel, sizes), out_shape=out_shape...  69.8 us
    pallas_call x1, Pallas kernels, tail(): pl.pallas_call(finish_kernel, out_shape=out_shape, in_specs=[vmem] * 3, o...  1.48 us

profile of v2, /device:TPU:0, one launch (start us, length us, event | category | flops | bytes accessed | tf_op | source)
XLA Modules:
  0.0 73.2 jit_solution(17725955234857858996)
XLA Ops:
  0.6 1.3 %reshape.33 = f32[2048]{0:T(1024)} convert(bf16[2048]{0:T(1024)(128)(2,1)} %param.21) | non-fusion elementwise | flops 2048 | bytes 12288 | tf_op jit(solution)/shard_map/reshape | solution.py:589
  1.9 69.8 %shard_map.148 = (bf16[16,2048]{1,0:T(8,128)(2,1)}, f32[1,128]{1,0:T(1,128)}, f32[1,128]{1,0:T(1,128)}) custom-call(bf16[16,16,128]{2,1,0:T(8,128)(2,1)} %probe_ref.1, bf16[16,2,512,128]{3,2,1,0:T(8,128)(2,1)} %keys_hbm.1, bf16[16,2,512,128]{3,2,1,0:T(8,128)(2,1)} %values_hbm.1, bf16[16,2,128]{2,1,0:T(2,128)(2,1)} %own_key_ref.1, ...), custom_call_target="tpu_custom_call" | custom-call | tf_op jit(solution)/shard_map/pallas_call | solution.py:534
  71.7 1.5 %shard_map.149 = (bf16[16,2048]{1,0:T(8,128)(2,1)}, f32[1,128]{1,0:T(1,128)}, f32[1,128]{1,0:T(1,128)}) custom-call(bf16[16,2048]{1,0:T(8,128)(2,1)} %get-tuple-element.9.hidden_in, f32[1,128]{1,0:T(1,128)} %get-tuple-element.10.targets_in, f32[1,128]{1,0:T(1,128)} %get-tuple-element.11.surprise_in), custom_call_target="tpu_custom_call" | custom-call | tf_op jit(solution)/shard_map/pallas_call | solution.py:595

commit v3 on v2

--- a/solution.py
+++ b/solution.py
@@ -47,8 +47,7 @@
     part,
     incoming,
     skip_block,
-    gain_block,
-    hidden_block,
+    gains,
     square_sums,
     state,
     logits,
@@ -62,8 +61,6 @@
     skip_recv,
     gain_send,
     gain_recv,
-    back_send,
-    back_recv,
     square_sems,
     part_send,
     part_recv,
@@ -84,6 +81,7 @@
     cache_len = keys.shape[2]
     rows = every_attn.shape[0]
     block_rows = rows // T
+    halves, half_rows = incoming.shape[1:3]
     width = mixing.shape[1]
     vocab_local = lexicon.shape[1]
 
@@ -111,7 +109,6 @@
             load.start()
 
     load_mixing.start()
-    load_lexicon.start()
 
     def wrap(position, size):
         return jnp.where(position >= size, position - size, position)
@@ -196,6 +193,7 @@
     for h in range(heads):
         attn_ref[:, h * head_dim : (h + 1) * head_dim] = row_attn[:, h, :].astype(jnp.bfloat16)
 
+    load_lexicon.start()
     pl.semaphore_wait(barrier, N - 1)
 
     def push(src, dst, send_sem, recv_sem, device):
@@ -254,20 +252,22 @@
                 skip_recv.at[home_slot],
                 (dest // R, home_t, dest % R),
             )
-            push(
-                gain_ref.at[j],
-                gain_block.at[home_slot],
-                gain_send.at[j],
-                gain_recv.at[home_slot],
-                (dest // R, home_t, dest % R),
-            )
 
         @pl.when(jnp.logical_not(away))
         def _():
             pltpu.make_async_copy(source, skip_rows(home_slot), skip_recv.at[home_slot]).start()
-            pltpu.make_async_copy(
-                gain_ref.at[j], gain_block.at[home_slot], gain_recv.at[home_slot]
-            ).start()
+
+    gains[pl.ds(t * fold, fold)] = gain_ref[...]
+    for j in range(1, T):
+        sends.append(
+            push(
+                gain_ref,
+                gains.at[pl.ds(t * fold, fold)],
+                gain_send.at[j],
+                gain_recv.at[t],
+                (g, (t + j) % T, r),
+            )
+        )
 
     for n, (a, b) in enumerate(peers):
         source = peer_from(a, b) + core
@@ -296,42 +296,72 @@
             every_attn[...], mixing[:, span], preferred_element_type=jnp.float32
         )
 
-    def block_of(index):
-        return pl.ds(pl.multiple_of(index * block_rows, block_rows), block_rows)
-
-    for j in range(1, T):
-        to_t = (t + j) % T
-        sends.append(
-            push(
-                part.at[block_of(to_t), :],
-                incoming.at[t],
-                part_send.at[j],
-                part_recv.at[t],
-                (g, to_t, r),
+    def block_of(index, half):
+        start = pl.multiple_of((index * halves + half) * half_rows, half_rows)
+        return pl.ds(start, half_rows)
+
+    for half in range(halves):
+        for j in range(1, T):
+            to_t = (t + j) % T
+            sends.append(
+                push(
+                    part.at[block_of(to_t, half), :],
+                    incoming.at[t, half],
+                    part_send.at[j, half],
+                    part_recv.at[t, half],
+                    (g, to_t, r),
+                )
             )
-        )
     for j in range(fold):
         local_wait(skip_rows(j), skip_recv.at[j])
-        local_wait(gain_block.at[j], gain_recv.at[j])
-    total = part[block_of(t), :]
-    for j in range(1, T):
-        from_t = (t + j) % T
-        local_wait(incoming.at[from_t], part_recv.at[from_t])
-        total = total + incoming[from_t]
-    hidden = (skip_block[...].astype(jnp.float32) + total).astype(jnp.bfloat16)
-    hidden_block[...] = hidden
-
-    def back_target(j):
-        owner = t * fold + j
-        return owner, column // fold, column % fold
-
-    def hidden_slot(slot):
-        return hidden_ref.at[:, pl.ds(pl.multiple_of(slot * width, width), width)]
-
-    wide = hidden.astype(jnp.float32)
+
+    def state_block(col, index, half):
+        return state.at[col, block_of(index, half), :]
+
+    def spread(index, half):
+        block = state_block(column, index, half)
+        for a, b in peers:
+            to_g, to_r = peer_to(a, b)
+            push(block, block, plane_send, state_recv.at[column, index, half], (to_g, t, to_r))
+        push(block, block, plane_send, state_recv.at[column, index, half], sibling)
+
+    for half in range(halves):
+        total = part[block_of(t, half), :]
+        for j in range(1, T):
+            from_t = (t + j) % T
+            local_wait(incoming.at[from_t, half], part_recv.at[from_t, half])
+            total = total + incoming[from_t, half]
+        residual = skip_block[half * half_rows : (half + 1) * half_rows, :].astype(jnp.float32)
+        state[column, block_of(t, half), :] = (residual + total).astype(jnp.bfloat16)
+        block = state_block(column, t, half)
+        for j in range(1, T):
+            push(
+                block,
+                block,
+                column_send,
+                state_recv.at[column, t, half],
+                (g, (t + j) % T, r),
+            )
+        spread(t, half)
+
+    def arrive(col):
+        for half in range(halves):
+            for j in range(T):
+                from_t = (t + j) % T
+                local_wait(state_block(col, from_t, half), state_recv.at[col, from_t, half])
+
+    for half in range(halves):
+        for j in range(1, T):
+            from_t = (t + j) % T
+            local_wait(
+                state_block(column, from_t, half), state_recv.at[column, from_t, half]
+            )
+            spread(from_t, half)
+
+    wide = state[column].astype(jnp.float32)
     row_squares = jnp.sum(wide * wide, axis=1, keepdims=True)
-    diagonal = lax.broadcasted_iota(jnp.int32, (block_rows, 128), 1) == (
-        lax.broadcasted_iota(jnp.int32, (block_rows, 128), 0)
+    diagonal = lax.broadcasted_iota(jnp.int32, (rows, rows), 1) == (
+        lax.broadcasted_iota(jnp.int32, (rows, rows), 0)
     )
     square_sums[column] = jnp.sum(
         jnp.where(diagonal, row_squares, 0.0), axis=0, keepdims=True
@@ -346,94 +376,43 @@
                     square_sems.at[1],
                     (wrap(g + a, G), t, wrap(r + d, R)),
                 )
-    for j in range(fold):
-        owner, at_t, slot = back_target(j)
-        away = jnp.logical_or(owner != column, at_t != t)
-        source = hidden_block.at[pl.ds(j * own_rows, own_rows), :]
-
-        @pl.when(away)
-        def _():
-            push(
-                source,
-                hidden_slot(slot),
-                back_send.at[j],
-                back_recv.at[slot],
-                (owner // R, at_t, owner % R),
-            )
-
-        @pl.when(jnp.logical_not(away))
-        def _():
-            pltpu.make_async_copy(source, hidden_slot(slot), back_recv.at[slot]).start()
-
+    for j in range(1, T):
+        from_t = (t + j) % T
+        local_wait(gains.at[pl.ds(from_t * fold, fold)], gain_recv.at[from_t])
+    load_lexicon.wait()
     local_wait(square_sums.at[pl.ds(0, columns - 1)], square_sems.at[1])
     mean_square = jnp.sum(square_sums[...], axis=0) / (columns * width)
     scale = lax.rsqrt(
         jnp.sum(jnp.where(diagonal, mean_square, 0.0), axis=1, keepdims=True) + 1e-05
     )
-    state[column, block_of(t), :] = (wide * scale * gain_block[0]).astype(jnp.bfloat16)
-
-    def state_block(col, index):
-        return state.at[col, block_of(index), :]
-
-    def spread(index):
-        for a, b in peers:
-            to_g, to_r = peer_to(a, b)
-            push(
-                state_block(column, index),
-                state_block(column, index),
-                plane_send,
-                state_recv.at[column, index],
-                (to_g, t, to_r),
-            )
-        push(
-            state_block(column, index),
-            state_block(column, index),
-            plane_send,
-            state_recv.at[column, index],
-            sibling,
-        )
-
-    for j in range(1, T):
-        push(
-            state_block(column, t),
-            state_block(column, t),
-            column_send,
-            state_recv.at[column, t],
-            (g, (t + j) % T, r),
-        )
-    spread(t)
-    load_lexicon.wait()
     logits[...] = jnp.zeros_like(logits)
 
     def head(col):
+        normed = (state[col].astype(jnp.float32) * scale * gains[col]).astype(jnp.bfloat16)
         block = lexicon[pl.ds(pl.multiple_of(col * width, width), width), :]
-        logits[...] += jnp.dot(state[col], block, preferred_element_type=jnp.float32)
-
-    for j in range(1, T):
-        from_t = (t + j) % T
-        local_wait(state_block(column, from_t), state_recv.at[column, from_t])
-        spread(from_t)
+        logits[...] += jnp.dot(normed, block, preferred_element_type=jnp.float32)
+
     head(column)
-    for j in range(T):
-        from_t = (t + j) % T
-        local_wait(state_block(twin, from_t), state_recv.at[twin, from_t])
+    arrive(twin)
     head(twin)
 
     @pl.loop(1, G * pairs)
     def _(step):
         source = peer_from(step // pairs, step % pairs)
-        for j in range(T):
-            from_t = (t + j) % T
-            block = state_block(source + core, from_t)
-            local_wait(block, state_recv.at[source + core, from_t])
-            push(block, block, pair_send, state_recv.at[source + core, from_t], sibling)
+        for half in range(halves):
+            for j in range(T):
+                from_t = (t + j) % T
+                block = state_block(source + core, from_t, half)
+                sem = state_recv.at[source + core, from_t, half]
+                local_wait(block, sem)
+                push(block, block, pair_send, sem, sibling)
         head(source + core)
-        for j in range(T):
-            from_t = (t + j) % T
-            local_wait(
-                state_block(source + other, from_t), state_recv.at[source + other, from_t]
-            )
+        arrive(source + other)
         head(source + other)
+
+    own_span = pl.ds(pl.multiple_of(column * own_rows, own_rows), own_rows)
+    for j in range(fold):
+        hidden_ref[:, j * width : (j + 1) * width] = state[t * fold + j, own_span, :]
 
     odds = logits[...].T * sharp_ref[...]
     entry = me * vocab_local + lax.broadcasted_iota(jnp.int32, odds.shape, 0)
@@ -486,15 +465,6 @@
         @pl.when(away)
         def _():
             local_wait(skip_ref.at[:, pl.ds(j * width, width)], skip_send.at[j])
-            local_wait(gain_ref.at[j], gain_send.at[j])
-
-        owner, at_t, slot = back_target(j)
-
-        @pl.when(jnp.logical_or(owner != column, at_t != t))
-        def _():
-            local_wait(hidden_block.at[pl.ds(j * own_rows, own_rows), :], back_send.at[j])
-
-        local_wait(hidden_slot(j), back_recv.at[j])
 
     local_wait(square_sums.at[pl.ds(0, columns - 1)], square_sems.at[0])
     local_wait(state.at[0, pl.ds(0, (T - 1) * block_rows), :], column_send)
@@ -523,6 +493,7 @@
     depth = mixing.shape[0]
     features, vocab_local = lexicon.shape
     peers = columns // 2 - 1
+    halves = 2
     vmem = pl.BlockSpec(memory_space=pltpu.VMEM)
     hbm = pl.BlockSpec(memory_space=pl.ANY)
     dma = pltpu.SemaphoreType.DMA
@@ -545,11 +516,10 @@
             pltpu.VMEM(lexicon.shape, jnp.bfloat16),
             pltpu.VMEM((rows, depth), jnp.bfloat16),
             pltpu.VMEM((rows, width), jnp.float32),
-            pltpu.VMEM((T, block_rows, width), jnp.float32),
+            pltpu.VMEM((T, halves, block_rows // halves, width), jnp.float32),
             pltpu.VMEM((block_rows, width), jnp.bfloat16),
-            pltpu.VMEM((fold, 1, width), jnp.float32),
-            pltpu.VMEM((block_rows, width), jnp.bfloat16),
-            pltpu.VMEM((columns, 1, 128), jnp.float32),
+            pltpu.VMEM((columns, 1, width), jnp.float32),
+            pltpu.VMEM((columns, 1, rows), jnp.float32),
             pltpu.VMEM((columns, rows, width), jnp.bfloat16),
             pltpu.VMEM((rows, vocab_local), jnp.float32),
             pltpu.VMEM((N, 8, rows), jnp.float32),
@@ -560,17 +530,15 @@
             dma((columns,)),
             dma((fold,)),
             dma((fold,)),
-            dma((fold,)),
-            dma((fold,)),
-            dma((fold,)),
-            dma((fold,)),
-            dma((2,)),
             dma((T,)),
             dma((T,)),
+            dma((2,)),
+            dma((T, halves)),
+            dma((T, halves)),
             dma,
             dma,
             dma,
-            dma((columns, T)),
+            dma((columns, T, halves)),
             dma((2,)),
             dma((2,)),
         ],

time: 73.5 us -> 70.5 us (0.959)
  Pallas kernels: 71.3 us -> 68.3 us
    pallas_call x1, Pallas kernels: 69.8 us -> 66.9 us  [tail(): pl.pallas_call(functools.partial(tail_kernel, sizes), out_shape=out_shape...]
where the time goes in v3:
time: 70.5 us; the launch traced here: 70.3 us
  Pallas kernels  68.3 us (97%)
  other arithmetic  1.29 us (2%)
    pallas_call x1, Pallas kernels, tail(): pl.pallas_call(functools.partial(tail_kernel, sizes), out_shape=out_shape...  66.9 us
    pallas_call x1, Pallas kernels, tail(): pl.pallas_call(finish_kernel, out_shape=out_shape, in_specs=[vmem] * 3, o...  1.48 us

profile of v3, /device:TPU:0, one launch (start us, length us, event | category | flops | bytes accessed | tf_op | source)
XLA Modules:
  0.0 70.3 jit_solution(5585736570666010553)
XLA Ops:
  0.6 1.3 %reshape.33 = f32[2048]{0:T(1024)} convert(bf16[2048]{0:T(1024)(128)(2,1)} %param.21) | non-fusion elementwise | flops 2048 | bytes 12288 | tf_op jit(solution)/shard_map/reshape | solution.py:557
  1.9 66.9 %shard_map.148 = (bf16[16,2048]{1,0:T(8,128)(2,1)}, f32[1,128]{1,0:T(1,128)}, f32[1,128]{1,0:T(1,128)}) custom-call(bf16[16,16,128]{2,1,0:T(8,128)(2,1)} %probe_ref.1, bf16[16,2,512,128]{3,2,1,0:T(8,128)(2,1)} %keys_hbm.1, bf16[16,2,512,128]{3,2,1,0:T(8,128)(2,1)} %values_hbm.1, bf16[16,2,128]{2,1,0:T(2,128)(2,1)} %own_key_ref.1, ...), custom_call_target="tpu_custom_call" | custom-call | tf_op jit(solution)/shard_map/pallas_call | solution.py:505
  68.8 1.5 %shard_map.149 = (bf16[16,2048]{1,0:T(8,128)(2,1)}, f32[1,128]{1,0:T(1,128)}, f32[1,128]{1,0:T(1,128)}) custom-call(bf16[16,2048]{1,0:T(8,128)(2,1)} %get-tuple-element.9.hidden_in, f32[1,128]{1,0:T(1,128)} %get-tuple-element.10.targets_in, f32[1,128]{1,0:T(1,128)} %get-tuple-element.11.surprise_in), custom_call_target="tpu_custom_call" | custom-call | tf_op jit(solution)/shard_map/pallas_call | solution.py:563

commit v4 on v3

--- a/solution.py
+++ b/solution.py
@@ -51,8 +51,10 @@
     square_sums,
     state,
     logits,
-    stats,
-    kept_parts,
+    column_stats,
+    plane_stats,
+    column_kept,
+    plane_kept,
     cache_sems,
     load_sems,
     attn_send,
@@ -72,7 +74,6 @@
     kept_sems,
 ):
     G, T, R = sizes
-    N = G * T * R
     columns = G * R
     fold = columns // T
     pairs = R // 2
@@ -113,25 +114,27 @@
     def wrap(position, size):
         return jnp.where(position >= size, position - size, position)
 
-    def every_other(visit):
-        for a in range(G):
-            to_g = wrap(g + a, G)
-
-            @pl.loop(1 if a == 0 else 0, T)
-            def _(b):
-                to_t = wrap(t + b, T)
-                for d in range(R):
-                    visit((to_g, to_t, wrap(r + d, R)))
-
-        for d in range(1, R):
-            visit((g, t, wrap(r + d, R)))
-
+    partners = [(g, wrap(t + b, T), r) for b in range(1, T)]
+    partners += [
+        (wrap(g + a, G), t, wrap(r + d, R)) for a in range(G) for d in range(R) if (a, d) != (0, 0)
+    ]
     barrier = pltpu.get_barrier_semaphore()
-    every_other(
-        lambda device: pl.semaphore_signal(
-            barrier, inc=1, device_id=device, device_id_type=MESH
-        )
-    )
+    for device in partners:
+        pl.semaphore_signal(barrier, inc=1, device_id=device, device_id_type=MESH)
+
+    home_t = column // fold
+    home_slot = column % fold
+    homes = []
+    for j in range(fold):
+        dest = t * fold + j
+        away = jnp.logical_or(dest != column, home_t != t)
+        homes.append((away, (dest // R, home_t, dest % R)))
+
+        @pl.when(away)
+        def _():
+            pl.semaphore_signal(
+                barrier, inc=1, device_id=homes[j][1], device_id_type=MESH
+            )
 
     score_scale = 1.0 / math.sqrt(head_dim)
     share_of = heads // kv_heads
@@ -194,7 +197,10 @@
         attn_ref[:, h * head_dim : (h + 1) * head_dim] = row_attn[:, h, :].astype(jnp.bfloat16)
 
     load_lexicon.start()
-    pl.semaphore_wait(barrier, N - 1)
+    pl.semaphore_wait(
+        barrier, len(partners) + sum(jnp.where(away, 1, 0) for away, _ in homes)
+    )
+
 
     def push(src, dst, send_sem, recv_sem, device):
         copy = pltpu.make_async_remote_copy(
@@ -232,15 +238,11 @@
     )
     every_attn[pl.ds(pl.multiple_of(column * own_rows, own_rows), own_rows), :] = attn_ref[...]
 
-    home_t = column // fold
-    home_slot = column % fold
-
     def skip_rows(slot):
         return skip_block.at[pl.ds(pl.multiple_of(slot * own_rows, own_rows), own_rows), :]
 
     for j in range(fold):
-        dest = t * fold + j
-        away = jnp.logical_or(dest != column, home_t != t)
+        away, home = homes[j]
         source = skip_ref.at[:, pl.ds(j * width, width)]
 
         @pl.when(away)
@@ -250,7 +252,7 @@
                 skip_rows(home_slot),
                 skip_send.at[j],
                 skip_recv.at[home_slot],
-                (dest // R, home_t, dest % R),
+                home,
             )
 
         @pl.when(jnp.logical_not(away))
@@ -419,23 +421,37 @@
     token_part = jnp.sum(jnp.where(entry == chosen_ref[...], odds, 0.0), axis=0, keepdims=True)
     local_top = jnp.max(odds, axis=0, keepdims=True)
     local_total = jnp.sum(jnp.exp(odds - local_top), axis=0, keepdims=True)
-    stats[me] = jnp.concatenate(
-        [local_top, local_total, token_part, jnp.zeros((5, rows), jnp.float32)], axis=0
-    )
-
-    def share(buffer, sems):
-        every_other(
-            lambda device: push(
-                buffer.at[me], buffer.at[me], sems.at[0], sems.at[1], device
-            )
-        )
-        local_wait(buffer.at[pl.ds(0, N - 1)], sems.at[1])
-
-    share(stats, stats_sems)
-    tops = stats[:, 0, :]
-    top = jnp.max(tops, axis=0, keepdims=True)
-    sum_exp = jnp.sum(stats[:, 1, :] * jnp.exp(tops - top), axis=0, keepdims=True)
-    token_logit = jnp.sum(stats[:, 2, :], axis=0, keepdims=True)
+    spare = jnp.zeros((1, rows), jnp.float32)
+
+    def share_column(buffer, sems):
+        for j in range(1, T):
+            push(buffer.at[t], buffer.at[t], sems.at[0], sems.at[1], (g, wrap(t + j, T), r))
+        local_wait(buffer.at[pl.ds(0, T - 1)], sems.at[1])
+
+    def share_plane(buffer, sems):
+        for a in reversed(range(G)):
+            for d in reversed(range(R)):
+                if (a, d) != (0, 0):
+                    push(
+                        buffer.at[column],
+                        buffer.at[column],
+                        sems.at[0],
+                        sems.at[1],
+                        (wrap(g + a, G), t, wrap(r + d, R)),
+                    )
+        local_wait(buffer.at[pl.ds(0, columns - 1)], sems.at[1])
+
+    def merge(buffer):
+        tops = buffer[:, 0, :]
+        top = jnp.max(tops, axis=0, keepdims=True)
+        sum_exp = jnp.sum(buffer[:, 1, :] * jnp.exp(tops - top), axis=0, keepdims=True)
+        return top, sum_exp, jnp.sum(buffer[:, 2, :], axis=0, keepdims=True)
+
+    column_stats[t] = jnp.concatenate([local_top, local_total, token_part, spare], axis=0)
+    share_column(column_stats, stats_sems.at[0])
+    plane_stats[column] = jnp.concatenate([*merge(column_stats), spare], axis=0)
+    share_plane(plane_stats, stats_sems.at[1])
+    top, sum_exp, token_logit = merge(plane_stats)
     lognorm = top + jnp.log(sum_exp)
     mu = mu_ref[...]
     logp = odds - lognorm
@@ -443,9 +459,11 @@
     tail = jnp.exp(-jnp.abs(margin))
     weight = jnp.where(margin >= 0.0, 1.0, tail) / (1.0 + tail)
     kept_local = jnp.sum(jnp.exp(logp) * weight, axis=0, keepdims=True)
-    kept_parts[me] = kept_local
-    share(kept_parts, kept_sems)
-    kept = jnp.sum(kept_parts[...], axis=0)
+    column_kept[t] = kept_local
+    share_column(column_kept, kept_sems.at[0])
+    plane_kept[column] = jnp.sum(column_kept[...], axis=0)
+    share_plane(plane_kept, kept_sems.at[1])
+    kept = jnp.sum(plane_kept[...], axis=0)
     token_logp = token_logit - lognorm
     token_margin = cut_slope * (mu + token_logp / math.log(2.0))
     token_logw = (
@@ -460,9 +478,7 @@
     for copy in sends:
         copy.wait_send()
     for j in range(fold):
-        away = jnp.logical_or(t * fold + j != column, home_t != t)
-
-        @pl.when(away)
+        @pl.when(homes[j][0])
         def _():
             local_wait(skip_ref.at[:, pl.ds(j * width, width)], skip_send.at[j])
 
@@ -470,8 +486,10 @@
     local_wait(state.at[0, pl.ds(0, (T - 1) * block_rows), :], column_send)
     local_wait(state.at[pl.ds(0, len(peers) + 1)], plane_send)
     local_wait(state.at[pl.ds(0, len(peers))], pair_send)
-    local_wait(stats.at[pl.ds(0, N - 1)], stats_sems.at[0])
-    local_wait(kept_parts.at[pl.ds(0, N - 1)], kept_sems.at[0])
+    local_wait(column_stats.at[pl.ds(0, T - 1)], stats_sems.at[0, 0])
+    local_wait(plane_stats.at[pl.ds(0, columns - 1)], stats_sems.at[1, 0])
+    local_wait(column_kept.at[pl.ds(0, T - 1)], kept_sems.at[0, 0])
+    local_wait(plane_kept.at[pl.ds(0, columns - 1)], kept_sems.at[1, 0])
 
 
 def finish_kernel(hidden_in, targets_in, surprise_in, hidden_ref, targets_ref, surprise_ref):
@@ -482,7 +500,6 @@
 
 def tail(sizes, probe, keys, values, own_key, own_value, counts, mixing, skip, gain, lexicon, sharp, mu, chosen):
     G, T, R = sizes
-    N = G * T * R
     columns = G * R
     fold = columns // T
     own_rows, heads, head_dim = probe.shape
@@ -522,8 +539,10 @@
             pltpu.VMEM((columns, 1, rows), jnp.float32),
             pltpu.VMEM((columns, rows, width), jnp.bfloat16),
             pltpu.VMEM((rows, vocab_local), jnp.float32),
-            pltpu.VMEM((N, 8, rows), jnp.float32),
-            pltpu.VMEM((N, 1, rows), jnp.float32),
+            pltpu.VMEM((T, 4, rows), jnp.float32),
+            pltpu.VMEM((columns, 4, rows), jnp.float32),
+            pltpu.VMEM((T, 1, rows), jnp.float32),
+            pltpu.VMEM((columns, 1, rows), jnp.float32),
             dma((2, load_groups)),
             dma((2,)),
             dma((2 * peers + 1,)),
@@ -539,8 +558,8 @@
             dma,
             dma,
             dma((columns, T, halves)),
-            dma((2,)),
-            dma((2,)),
+            dma((2, 2)),
+            dma((2, 2)),
         ],
         compiler_params=pltpu.CompilerParams(
             collective_id=0, has_side_effects=True, vmem_limit_bytes=56 * 2**20

time: 70.5 us -> 72.4 us (1.027)
  Pallas kernels: 68.3 us -> 70.2 us
    pallas_call x1, Pallas kernels: 66.9 us -> 68.8 us  [tail(): pl.pallas_call(functools.partial(tail_kernel, sizes), out_shape=out_shape...]
where the time goes in v4:
time: 72.4 us; the launch traced here: 72.2 us
  Pallas kernels  70.2 us (97%)
  other arithmetic  1.29 us (2%)
    pallas_call x1, Pallas kernels, tail(): pl.pallas_call(functools.partial(tail_kernel, sizes), out_shape=out_shape...  68.8 us
    pallas_call x1, Pallas kernels, tail(): pl.pallas_call(finish_kernel, out_shape=out_shape, in_specs=[vmem] * 3, o...  1.48 us

profile of v4, /device:TPU:0, one launch (start us, length us, event | category | flops | bytes accessed | tf_op | source)
XLA Modules:
  0.0 72.2 jit_solution(16489684547611867151)
XLA Ops:
  0.6 1.3 %reshape.33 = f32[2048]{0:T(1024)} convert(bf16[2048]{0:T(1024)(128)(2,1)} %param.21) | non-fusion elementwise | flops 2048 | bytes 12288 | tf_op jit(solution)/shard_map/reshape | solution.py:576
  1.9 68.8 %shard_map.148 = (bf16[16,2048]{1,0:T(8,128)(2,1)}, f32[1,128]{1,0:T(1,128)}, f32[1,128]{1,0:T(1,128)}) custom-call(bf16[16,16,128]{2,1,0:T(8,128)(2,1)} %probe_ref.1, bf16[16,2,512,128]{3,2,1,0:T(8,128)(2,1)} %keys_hbm.1, bf16[16,2,512,128]{3,2,1,0:T(8,128)(2,1)} %values_hbm.1, bf16[16,2,128]{2,1,0:T(2,128)(2,1)} %own_key_ref.1, ...), custom_call_target="tpu_custom_call" | custom-call | tf_op jit(solution)/shard_map/pallas_call | solution.py:522
  70.7 1.5 %shard_map.149 = (bf16[16,2048]{1,0:T(8,128)(2,1)}, f32[1,128]{1,0:T(1,128)}, f32[1,128]{1,0:T(1,128)}) custom-call(bf16[16,2048]{1,0:T(8,128)(2,1)} %get-tuple-element.9.hidden_in, f32[1,128]{1,0:T(1,128)} %get-tuple-element.10.targets_in, f32[1,128]{1,0:T(1,128)} %get-tuple-element.11.surprise_in), custom_call_target="tpu_custom_call" | custom-call | tf_op jit(solution)/shard_map/pallas_call | solution.py:582
